TPU v7x, 32 devices: a whole 2x2x4 slice. The times are simulated.
32 devices in a mesh: chan: 8 (over z, x), win: 4 (over y, core).
Axes of the slice: x: 2, y: 2, z: 4, core: 2. Of those that a mesh axis runs over, the one named last changes fastest.
Arguments:
- spectra: bfloat16 [8, 128, 128, 2, 128], P('chan', None, 'win'), may hold values from -6 to 6
- counts: int32 [128, 8], P('win'), may hold values from 1 to 256
- partner: int32 [2, 8], replicated, may hold values from 0 to 7, as said below
Outputs:
- cross: bfloat16 [8, 2, 128, 128, 256], P('win', None, 'chan')
Inputs may be any that keep to these rules, and one draw needn't show every extreme that they name: Each row of partner is one cycle through all 8 blocks: a permutation with no block its own partner and no two blocks each other's partners.
All inputs are finite; a program needn't handle non-finite values.
Results may differ from a plain program's by a relative error of at most 0.015.
Values may be sent and summed in bfloat16 or wider, within the bound.
A program may use at most 128 MiB of HBM per device.

v0:
```python
import jax
import jax.numpy as jnp
from jax import lax
from jax.sharding import PartitionSpec as P

W_DEV = 32
NSAMP = 256


EPS = 1e-06


def stack_blocks(blocks, scale, mate_index, first, count):
    own = lax.dynamic_slice_in_dim(blocks, first, count, 0)
    mates = jnp.take(blocks, mate_index, axis=0)
    weighted = (scale[:, :, None, :, :, None, None] * own[:, None]).astype(jnp.bfloat16)
    rotated = jnp.stack([-mates[..., 1, :], mates[..., 0, :]], axis=-2)
    paired = jnp.stack([mates, rotated], axis=-2)
    return jnp.einsum(
        "nrfgwkc,nrfgwkod->nrfgcod", weighted, paired, preferred_element_type=jnp.float32
    )


def weights_of(tallies, partner):
    columns = tallies.astype(jnp.float32).T
    return jnp.minimum(columns[None], jnp.take(columns, partner, axis=0)) / NSAMP


def per_device(spectra, counts, partner):
    values = spectra.astype(jnp.float32)
    power = jnp.mean(jnp.sum(values * values, axis=3), axis=1)
    whitened = (values * lax.rsqrt(power + EPS)[:, None, :, None, :]).astype(jnp.bfloat16)
    mixed = lax.all_to_all(whitened, "chan", split_axis=1, concat_axis=0, tiled=True)
    nblocks = partner.shape[1]
    width = mixed.shape[4]
    local_bins = mixed.shape[1]
    rounds = partner.shape[0]
    groups = lax.axis_size("win")
    chosen = nblocks // groups
    first = lax.axis_index("win") * chosen
    gathered = lax.all_gather(mixed, "win", axis=2, tiled=True)
    tallies = lax.all_gather(counts, "win", axis=0, tiled=True)
    weight = weights_of(tallies, partner)
    norm = jnp.sqrt(jnp.sum(weight * weight, axis=2))
    blocks = gathered.reshape(nblocks, local_bins, groups, W_DEV, 2, width)
    own_scales = jnp.transpose(lax.dynamic_slice_in_dim(weight, first, chosen, 1), (1, 0, 2))
    scale = own_scales.reshape(chosen, rounds, groups, W_DEV)
    mate_index = jnp.transpose(lax.dynamic_slice_in_dim(partner, first, chosen, 1))
    partial_value = stack_blocks(blocks, scale, mate_index, first, chosen)
    partial_value = lax.optimization_barrier(partial_value.astype(jnp.bfloat16))
    total = jnp.sum(partial_value.astype(jnp.float32), axis=3)
    norm_rows = jnp.transpose(lax.dynamic_slice_in_dim(norm, first, chosen, 1))
    shaped = total.reshape(chosen, rounds, local_bins, width, 2 * width)
    result = shaped / norm_rows[:, :, None, None, None]
    return result.astype(jnp.bfloat16)


def solution(mesh):
    placed = (P("chan", None, "win", None, None), P("win", None), P())
    return jax.shard_map(
        per_device,
        mesh=mesh,
        in_specs=placed,
        out_specs=P("win", None, "chan", None, None),
        check_vma=False,
    )
```

profile of v0, /device:TPU:1, one launch (start us, length us, event | category | flops | bytes accessed | tf_op | source)
XLA Modules:
  0.0 202.9 jit_solution(14903796572689402253)
XLA Ops:
  6.5 0.0 all-gather.3.cloned.1.call-start
  6.5 3.8 %fusion.4 = f32[32,128]{1,0:T(8,128)S(1)} fusion(bf16[1,128,32,2,128]{4,3,2,1,0:T(2,128)(2,1)} %param.3), kind=kLoop, calls=%fused_computation.12 | loop fusion | flops 3141632 | bytes 2113536 | tf_op jit(solution)/shard_map/reduce_sum | solution.py:31
  10.4 3.8 %fusion.5 = bf16[1,128,32,2,128]{4,3,2,0,1:T(2,128)(2,1)S(1)} fusion(bf16[1,128,32,2,128]{4,3,2,1,0:T(2,128)(2,1)} %param.3, f32[32,128]{1,0:T(8,128)S(1)} %add_rsqrt_fusion), kind=kLoop, calls=%fused_computation.13 | loop fusion | flops 3145728 | bytes 4210688 | tf_op jit(solution)/shard_map/convert_element_type | solution.py:32
  14.2 53.5 %all_to_all.12 = bf16[1,128,32,2,128]{4,3,2,0,1:T(2,128)(2,1)S(1)} all-to-all(bf16[1,128,32,2,128]{4,3,2,0,1:T(2,128)(2,1)S(1)} %fusion.5), channel_id=1, replica_groups=mesh['chan'=8,'win'=4] {'chan'}, dimensions={1} | all-to-all | bytes 4194304 | tf_op jit(solution)/shard_map/all_to_all | solution.py:33
  67.7 1.9 copy.36
  69.6 0.0 all-gather.3.cloned.1.call-update
  69.7 0.1 reshape.48
  69.7 0.1 compare_and_fusion
  69.8 0.1 copy.38
  69.9 0.1 copy.39
  70.0 0.1 reshape.56
  70.1 0.0 copy-done.1
  70.1 6.9 %all-gather = s32[4,32,8]{1,2,0:T(8,128)S(1)} all-gather(s32[1,32,8]{1,2,0:T(8,128)S(1)} %bitcast.48), channel_id=1, replica_groups=mesh['chan'=8,'win'=4] {'win'}, dimensions={0}, use_global_device_ids=true | all-gather | bytes 5120 | tf_op jit(solution)/shard_map/all_gather | solution.py:42
  77.1 0.1 reshape.69
  77.2 0.6 gather_fusion
  77.7 0.2 multiply_reduce_fusion
  77.9 0.1 dynamic-slice_bitcast_fusion.1
  78.0 0.1 copy.43
  78.1 0.1 mul.33
  78.2 50.5 %all-gather.3.cloned.1.call-done = bf16[8,16,128,2,128]{4,2,3,1,0:T(8,128)(2,1)} async-done(((bf16[8,16,32,2,128]{4,2,3,1,0:T(8,128)(2,1)}), bf16[8,16,128,2,128]{4,2,3,1,0:T(8,128)(2,1)}) %all-gather.3.cloned.1.call-update) | async-done | bytes 8388624 | tf_op jit(solution)/shard_map/all_gather | solution.py:41
  128.7 9.2 %copy.40 = bf16[8,16,4,32,2,128]{5,3,4,2,1,0:T(8,128)(2,1)} copy(bf16[8,16,4,32,2,128]{5,3,2,4,1,0:T(8,128)(2,1)} %bitcast.43) | data formatting | bytes 16777216 | tf_op jit(solution)/shard_map/reshape | solution.py:45
  137.8 6.5 %gather_fusion.1 = bf16[4,16,4,32,2,128]{5,3,4,2,1,0:T(8,128)(2,1)} fusion(bf16[8,16,4,32,2,128]{5,3,4,2,1,0:T(8,128)(2,1)} %copy.40, s32[1024]{0:T(1024)S(1)} %pad_clamp_fusion), kind=kCustom, calls=%fused_computation.1 | custom fusion | bytes 8388624 | tf_op jit(solution)/shard_map/jit(_take)/gather | solution.py:15
  144.3 2.8 %broadcast_select_fusion = bf16[2,2,16,4,32,2,128]{6,4,5,3,2,1,0:T(8,128)(2,1)S(1)} fusion(bf16[2,2,16,4,32,2,128]{6,4,5,3,2,1,0:T(8,128)(2,1)} %bitcast.41, pred[2,2]{1,0:T(4,128)(4,1)S(1)} %copy.38), kind=kLoop, calls=%fused_computation.18 | loop fusion | flops 2097152 | bytes 8388612 | tf_op jit(solution)/shard_map/jit(_take)/select_n | solution.py:15
  147.1 0.6 copy-done
  147.8 0.5 broadcast_select_fusion.1
  148.2 0.4 slice_negate_fusion
  148.6 2.4 %maximum_bitcast_fusion = bf16[2,2,16,4,32,2,1,128]{7,4,5,6,3,2,1,0:T(8,128)(2,1)} fusion(bf16[2,2,16,4,32,1,128]{6,4,5,3,2,1,0:T(8,128)(2,1)S(1)} %get-tuple-element.10, bf16[2,2,16,4,32,1,128]{6,4,5,3,2,1,0:T(8,128)(2,1)S(1)} %get-tuple-element.9), kind=kLoop, calls=%fused_computation.15 | loop fusion | flops 2097152 | bytes 8388608 | tf_op jit(solution)/shard_map/stack | solution.py:18
  151.0 10.7 %bitcast_convert_fusion = bf16[2,2,16,4,128,2,128]{6,4,5,3,2,1,0:T(8,128)(2,1)} fusion(bf16[2,2,16,4,32,2,1,128]{7,4,5,6,3,2,1,0:T(8,128)(2,1)} %maximum_bitcast_fusion, bf16[2,2,16,4,32,2,1,128]{7,4,5,6,3,2,1,0:T(8,128)(2,1)S(1)} %broadcast_select_fusion.1, f32[2,2,4,32]{3,2,0,1:T(4,128)S(1)} %mul.33, bf16[8,16,4,32,2,128]{5,3,2,4,1,0:T(8,128)(2,1)} %bitcast.44, ...), kind=kOutput, calls=%fused_computation.2 | convolution fusion | flops 1104150528 | bytes 27265028 | tf_op jit(solution)/shard_map/nrfgwkc,nrfgwkod->nrfgcod/dot_general | solution.py:19
  161.7 13.0 %convert_reduce_fusion = f32[2,2,16,128,2,128]{5,3,4,2,1,0:T(8,128)} fusion(bf16[2,2,16,4,128,2,128]{6,4,5,3,2,1,0:T(8,128)(2,1)} %bitcast_convert_fusion), kind=kLoop, calls=%fused_computation.3 | loop fusion | flops 14680064 | bytes 25165824 | tf_op jit(solution)/shard_map/reduce_sum | solution.py:51
  174.7 8.7 %copy.42 = f32[2,2,16,128,2,128]{3,5,4,2,1,0:T(8,128)} copy(f32[2,2,16,128,2,128]{5,3,4,2,1,0:T(8,128)} %convert_reduce_fusion) | data formatting | bytes 16777216 | tf_op jit(solution)/shard_map/reduce_sum | solution.py:51
  183.4 6.5 %fusion.3 = bf16[2,2,16,128,256]{3,4,2,1,0:T(8,128)(2,1)} fusion(f32[2,2,16,128,2,128]{3,5,4,2,1,0:T(8,128)} %copy.42, f32[2,2]{1,0:T(2,128)S(1)} %copy.43), kind=kLoop, calls=%fused_computation.8 | loop fusion | flops 4194304 | bytes 12582928 | tf_op jit(solution)/shard_map/convert_element_type | solution.py:55
  189.9 6.2 %copy.44 = bf16[2,2,16,128,256]{4,3,2,1,0:T(8,128)(2,1)} copy(bf16[2,2,16,128,256]{3,4,2,1,0:T(8,128)(2,1)} %fusion.3) | data formatting | bytes 8388608 | tf_op jit(solution)/shard_map/convert_element_type | solution.py:55
  (13 shorter events, 0.1 us)
Async XLA Ops:
  6.5 122.1 %all-gather.3.cloned.1.call-start = ((), (), s32[]{:S(2)}) async-start(), calls=%async_computation.1 | async-start | bytes 10485760 | tf_op jit(solution)/shard_map/all_gather | solution.py:41
  67.7 1.9 copy-start.2
  67.7 2.4 %copy-start.1 = (s32[32,8]{0,1:T(8,128)S(1)}, s32[32,8]{0,1:T(8,128)}, u32[]{:S(2)}) copy-start(s32[32,8]{0,1:T(8,128)} %param.4) | copy-start | bytes 3076
  144.3 3.4 %copy-start = (bf16[4,16,4,32,2,128]{5,3,4,2,1,0:T(8,128)(2,1)S(1)}, bf16[4,16,4,32,2,128]{5,3,4,2,1,0:T(8,128)(2,1)}, u32[]{:S(2)}) copy-start(bf16[4,16,4,32,2,128]{5,3,4,2,1,0:T(8,128)(2,1)} %gather_fusion.1) | copy-start | bytes 12582916
Sparse Core Ops, SparseCore 0:
  69.8 58.8 all-gather.2
where the time goes:
time: 204 us; the launch traced here: 203 us
  blocking collectives  60.5 us (30%)
  waiting for transfers between devices  50.5 us (25%)
  local copies, waits for them, and re-layouts  34.4 us (17%)
  other arithmetic  33.4 us (16%)
  between operations  13.5 us (7%)
  matrix products  10.7 us (5%)
    all_to_all x1, blocking collectives, per_device(): lax.all_to_all(whitened, 'chan', split_axis=1, concat_axis=0, tiled=True)  53.5 us
    all_gather x1, waiting for transfers between devices, per_device(): gathered = lax.all_gather(mixed, 'win', axis=2, tiled=True)  50.5 us
    reduce_sum x1, other arithmetic, per_device(): total = jnp.sum(partial_value.astype(jnp.float32), axis=3)  13 us
    dot_general x1, matrix products, stack_blocks(): jnp.einsum('nrfgwkc,nrfgwkod->nrfgcod', weighted, paired, preferred_eleme...  10.7 us
    reshape x1, local copies, waits for them, and re-layouts, per_device(): blocks = gathered.reshape(nblocks, local_bins, groups, W_DEV, 2, width)  9.15 us
    reduce_sum x1, local copies, waits for them, and re-layouts, per_device(): total = jnp.sum(partial_value.astype(jnp.float32), axis=3)  8.71 us
    all_gather x1, blocking collectives, per_device(): tallies = lax.all_gather(counts, 'win', axis=0, tiled=True)  6.95 us
    convert_element_type x1, other arithmetic, per_device(): return result.astype(jnp.bfloat16)  6.51 us
  transfers between devices with their start and end apart: 1, of which 1 were waited for; matrix products, arithmetic and copies ran while one was open for 1% of the time, Pallas kernels for 0%

commit v1 on v0

v1 whole, which is shorter than its diff:
```python
import functools

import jax
import jax.numpy as jnp
from jax import lax
from jax.experimental import pallas as pl
from jax.experimental.pallas import tpu as pltpu
from jax.sharding import PartitionSpec as P

NSAMP = 256
EPS = 1e-06
LANES = 128
MESH = pl.DeviceIdType.MESH


def flip(index, bits):
    out, place = index, 1
    while place <= bits:
        if bits & place:
            out = out + place * (1 - 2 * ((index // place) % 2))
        place *= 2
    return out


def kernel(cfg, x_ref, counts_ref, partner_ref, out_ref, *scratch):
    nchan, groups, nsub, per_sub, chosen, rounds, windows, width = cfg
    (send, tall, raw, wgt, inv, stage, sem_as, sem_ar, sem_ys, sem_yr, sem_bs, sem_br,
     sem_cs, sem_cr, sem_ts, sem_tr, sem_out) = scratch[:17]
    held = scratch[17:]
    bins = nsub * per_sub
    total_bins = nchan * bins
    me = lax.axis_index("chan")
    mine = lax.axis_index("win")
    across, beside = flip(mine, 2), flip(mine, 1)
    rows = 2 * windows

    barrier = pltpu.get_barrier_semaphore()
    for d in range(1, nchan):
        pl.semaphore_signal(barrier, 1, device_id={"chan": flip(me, d)}, device_id_type=MESH)
    for d in range(1, groups):
        pl.semaphore_signal(barrier, 1, device_id={"win": flip(mine, d)}, device_id_type=MESH)

    def to_bins(s, d):
        return pltpu.make_async_remote_copy(
            src_ref=send.at[s, flip(me, d)], dst_ref=held[s].at[me, mine],
            send_sem=sem_as.at[s, d], recv_sem=sem_ar.at[s, d],
            device_id={"chan": flip(me, d)}, device_id_type=MESH)

    def to_across(s, d):
        block = held[s].at[flip(me, d), mine]
        return pltpu.make_async_remote_copy(
            src_ref=block, dst_ref=block, send_sem=sem_ys.at[s, d], recv_sem=sem_yr.at[s, d],
            device_id={"win": across}, device_id_type=MESH)

    def to_beside(s, d):
        block = held[s].at[flip(me, d), mine]
        return pltpu.make_async_remote_copy(
            src_ref=block, dst_ref=block, send_sem=sem_bs.at[s, d], recv_sem=sem_br.at[s, d],
            device_id={"win": beside}, device_id_type=MESH)

    def relay(s, d):
        block = held[s].at[flip(me, d), across]
        return pltpu.make_async_remote_copy(
            src_ref=block, dst_ref=block, send_sem=sem_cs.at[s, d], recv_sem=sem_cr.at[s, d],
            device_id={"win": beside}, device_id_type=MESH)

    def tallies(d):
        return pltpu.make_async_remote_copy(
            src_ref=tall.at[mine], dst_ref=tall.at[mine],
            send_sem=sem_ts.at[d], recv_sem=sem_tr.at[d],
            device_id={"win": flip(mine, d)}, device_id_type=MESH)

    def store_out(s):
        return pltpu.make_async_copy(
            stage.at[s], out_ref.at[:, :, pl.ds(s * per_sub, per_sub)], sem_out.at[s])

    def add_power(f, acc):
        v = x_ref[f].astype(jnp.float32)
        return acc + v * v

    acc = lax.fori_loop(0, total_bins, add_power, jnp.zeros((rows, width), jnp.float32), unroll=4)
    raw[0] = acc
    power = (raw[0, pl.ds(0, windows, stride=2), :] + raw[0, pl.ds(1, windows, stride=2), :]) * (1.0 / total_bins)
    scale = lax.rsqrt(power + EPS)

    def whiten(s):
        def one(j, carry):
            for q in range(per_sub):
                raw[q] = x_ref[j * bins + s * per_sub + q].astype(jnp.float32)
            for q in range(per_sub):
                for k in range(2):
                    part = raw[q, pl.ds(k, windows, stride=2), :] * scale
                    send[s, j, q, pl.ds(k * windows, windows), :] = part.astype(jnp.bfloat16)
            return carry

        lax.fori_loop(0, nchan, one, 0)
        held[s][me, mine] = send[s, me]

    tall[mine] = jnp.zeros((windows, LANES), jnp.float32)
    tall[mine, :, pl.ds(0, counts_ref.shape[1])] = counts_ref[...].astype(jnp.float32)

    whiten(0)
    pl.semaphore_wait(barrier, nchan - 1 + groups - 1)
    for d in range(nchan - 1, 0, -1):
        to_bins(0, d).start()
    for d in range(1, groups):
        tallies(d).start()
    for s in range(1, nsub):
        whiten(s)
        if s < AHEAD:
            for d in range(nchan - 1, 0, -1):
                to_bins(s, d).start()

    def weights():
        for d in range(1, groups):
            tallies(d).wait_recv()
        c = tall[...].reshape(groups * windows, LANES)
        lane = lax.broadcasted_iota(jnp.int32, c.shape, 1)
        first = mine * chosen

        def column(a):
            return jnp.sum(jnp.where(lane == a, c, 0.0), axis=1, keepdims=True)

        def one(n, carry):
            own = column(first + n)
            for r in range(rounds):
                w = jnp.minimum(own, column(partner_ref[r, first + n])) * (1.0 / NSAMP)
                w = jnp.broadcast_to(w, (groups * windows, width))
                wgt[n, r] = w.astype(jnp.bfloat16)
                norm = lax.rsqrt(jnp.sum(w * w, axis=0, keepdims=True))
                inv[n, r] = jnp.broadcast_to(norm, (8, width))
            return carry

        lax.fori_loop(0, chosen, one, 0)

    def planes(s, block, q):
        return [
            jnp.concatenate(
                [held[s][block, g, q, pl.ds(k * windows, windows), :] for g in range(groups)], axis=0)
            for k in range(2)
        ]

    def unit(s, u):
        n, q = u // per_sub, u % per_sub
        a = mine * chosen + n
        re, im = planes(s, a, q)
        re, im = re.T, im.T
        lhs = jnp.concatenate(
            [jnp.concatenate([re, im], axis=1), jnp.concatenate([im, -re], axis=1)], axis=0)
        mates = []
        for r in range(rounds):
            w = wgt[n, r]
            mre, mim = planes(s, partner_ref[r, a], q)
            mates.append(jnp.concatenate([mre * w, mim * w], axis=0))
        rhs = jnp.concatenate(mates, axis=1)
        res = jnp.dot(lhs, rhs, preferred_element_type=jnp.float32)
        for r in range(rounds):
            norm = inv[n, r, pl.ds(0, 1), :]
            for k in range(2):
                tile = res[k * width:(k + 1) * width, r * width:(r + 1) * width] * norm
                stage[s, n, r, q, :, pl.ds(k * width, width)] = tile.astype(jnp.bfloat16)

    units = chosen * per_sub

    def compute(s, low, high):
        lax.fori_loop(low, high, lambda u, carry: (unit(s, u), carry)[1], 0)

    def settle(s):
        for d in range(nchan):
            to_beside(s, d).wait_recv()
            relay(s, d).wait_recv()

    late = nchan // 2
    previous = None
    for s in range(nsub):
        for d in range(nchan):
            if d:
                to_bins(s, d).wait_recv()
            to_across(s, d).start()
            to_beside(s, d).start()
            if d and s + AHEAD < nsub:
                to_bins(s + AHEAD, nchan - d).start()
            if previous is not None:
                to_across(*previous).wait_recv()
                relay(*previous).start()
            previous = (s, d)
            if s == 0 and d == nchan - 1:
                weights()
            if s and d >= late:
                if d == late:
                    settle(s - 1)
                step = d - late
                compute(s - 1, step * units // (nchan - late), (step + 1) * units // (nchan - late))
        if s:
            store_out(s - 1).start()
    to_across(*previous).wait_recv()
    relay(*previous).start()
    settle(nsub - 1)
    compute(nsub - 1, 0, units)
    store_out(nsub - 1).start()

    for d in range(1, groups):
        tallies(d).wait_send()
    for s in range(nsub):
        for d in range(nchan):
            if d:
                to_bins(s, d).wait_send()
            to_across(s, d).wait_send()
            to_beside(s, d).wait_send()
            relay(s, d).wait_send()
    for s in range(nsub):
        store_out(s).wait()


AHEAD = 2


def per_device(nchan, groups, spectra, counts, partner):
    _, total_bins, windows, parts, width = spectra.shape
    rounds, nblocks = partner.shape
    bins = total_bins // nchan
    chosen = nblocks // groups
    nsub = 4 if bins % 4 == 0 else bins
    per_sub = bins // nsub
    cfg = (nchan, groups, nsub, per_sub, chosen, rounds, windows, width)
    x = spectra.reshape(total_bins, windows * parts, width)
    dma = pltpu.SemaphoreType.DMA
    flops = 2 * chosen * rounds * bins * width * (2 * width) * (2 * groups * windows)
    return pl.pallas_call(
        functools.partial(kernel, cfg),
        out_shape=jax.ShapeDtypeStruct((chosen, rounds, bins, width, 2 * width), jnp.bfloat16),
        in_specs=[
            pl.BlockSpec(memory_space=pltpu.VMEM),
            pl.BlockSpec(memory_space=pltpu.VMEM),
            pl.BlockSpec(memory_space=pltpu.SMEM),
        ],
        out_specs=pl.BlockSpec(memory_space=pl.ANY),
        scratch_shapes=[
            pltpu.VMEM((nsub, nchan, per_sub, 2 * windows, width), jnp.bfloat16),
            pltpu.VMEM((groups, windows, LANES), jnp.float32),
            pltpu.VMEM((per_sub, 2 * windows, width), jnp.float32),
            pltpu.VMEM((chosen, rounds, groups * windows, width), jnp.bfloat16),
            pltpu.VMEM((chosen, rounds, 8, width), jnp.float32),
            pltpu.VMEM((nsub, chosen, rounds, per_sub, width, 2 * width), jnp.bfloat16),
        ]
        + [dma((nsub, nchan))] * 8
        + [dma((groups,))] * 2
        + [dma((nsub,))]
        + [pltpu.VMEM((nblocks, groups, per_sub, 2 * windows, width), jnp.bfloat16)] * nsub,
        compiler_params=pltpu.CompilerParams(
            collective_id=0, has_side_effects=True, vmem_limit_bytes=48 * 1024 * 1024),
        cost_estimate=pl.CostEstimate(flops=flops, bytes_accessed=8 << 20, transcendentals=0),
    )(x, counts, partner)


def solution(mesh):
    sizes = dict(mesh.shape)
    placed = (P("chan", None, "win", None, None), P("win", None), P())
    return jax.shard_map(
        functools.partial(per_device, sizes["chan"], sizes["win"]),
        mesh=mesh,
        in_specs=placed,
        out_specs=P("win", None, "chan", None, None),
        check_vma=False,
    )
```

time: 204 us -> 96.6 us (0.47)
  Pallas kernels: 0 us -> 88.7 us
  blocking collectives: 60.5 us -> 0 us
  waiting for transfers between devices: 50.5 us -> 0 us
  other arithmetic: 33.4 us -> 0 us
  local copies, waits for them, and re-layouts: 34.4 us -> 7.73 us
  between operations: 13.5 us -> 0.01 us
  matrix products: 10.7 us -> 0 us
    pallas_call x0 -> x1, Pallas kernels: none -> 88.7 us  [per_device(): pl.pallas_call(functools.partial(kernel, cfg), out_shape=jax.ShapeDtypeSt...]
    all_to_all x1 -> x0, blocking collectives: 53.5 us -> none  [per_device(): lax.all_to_all(whitened, 'chan', split_axis=1, concat_axis=0, tiled=True)]
    all_gather x1 -> x0, waiting for transfers between devices: 50.5 us -> none  [per_device(): gathered = lax.all_gather(mixed, 'win', axis=2, tiled=True)]
    reduce_sum x3 -> x0, other arithmetic: 16.9 us -> none  [the longest x1 13 us: per_device(): total = jnp.sum(partial_value.astype(jnp.float32), axis=3)]
    dot_general x1 -> x0, matrix products: 10.7 us -> none  [stack_blocks(): jnp.einsum('nrfgwkc,nrfgwkod->nrfgcod', weighted, paired, preferred_eleme...]
    convert_element_type x3 -> x0, other arithmetic: 10.3 us -> none  [the longest x1 6.51 us: per_device(): return result.astype(jnp.bfloat16)]
    reshape x1 -> x0, local copies, waits for them, and re-layouts: 9.15 us -> none  [per_device(): blocks = gathered.reshape(nblocks, local_bins, groups, W_DEV, 2, width)]
    reduce_sum x1 -> x0, local copies, waits for them, and re-layouts: 8.71 us -> none  [per_device(): total = jnp.sum(partial_value.astype(jnp.float32), axis=3)]
  transfers between devices with their start and end apart: 1 -> 0, of which waited for: 1 -> 0; matrix products, arithmetic and copies ran while one was open for 1% -> 0% of each run, Pallas kernels for 0% -> 0%
where the time goes in v1:
time: 96.6 us; the launch traced here: 96.4 us
  Pallas kernels  88.7 us (92%)
  local copies, waits for them, and re-layouts  7.73 us (8%)
    pallas_call x1, Pallas kernels, per_device(): pl.pallas_call(functools.partial(kernel, cfg), out_shape=jax.ShapeDtypeSt...  88.7 us
    unnamed x6, local copies, waits for them, and re-layouts  7.73 us

profile of v1, /device:TPU:1, one launch (start us, length us, event | category | flops | bytes accessed | tf_op | source)
XLA Modules:
  0.0 96.4 jit_solution(16901811586491623903)
XLA Ops:
  0.0 0.8 copy.4.counts_ref
  0.8 0.0 copy-start
  0.8 1.6 %copy-done = bf16[1,128,32,2,128]{4,3,2,1,0:T(2,128)(2,1)S(1)} copy-done((bf16[1,128,32,2,128]{4,3,2,1,0:T(2,128)(2,1)S(1)}, bf16[1,128,32,2,128]{4,3,2,1,0:T(2,128)(2,1)}, u32[]{:S(2)}) %copy-start) | copy-done | bytes 2097176
  2.4 0.0 copy-start.1
  2.4 0.7 copy-done.1
  3.0 88.7 %shard_map.37 = bf16[2,2,16,128,256]{4,3,2,1,0:T(8,128)(2,1)} custom-call(bf16[128,64,128]{2,1,0:T(8,128)(2,1)S(1)} %bitcast.1, s32[32,8]{1,0:T(8,128)S(1)} %copy.4.counts_ref, s32[2,8]{1,0:T(2,128)S(1)} %copy-done.1), custom_call_target="tpu_custom_call" | custom-call | flops 1073741824 | bytes 8388608 | tf_op jit(solution)/shard_map/pallas_call | solution.py:229
  91.7 4.7 %copy.6 = bf16[2,2,16,128,256]{4,3,2,1,0:T(8,128)(2,1)} copy(bf16[2,2,16,128,256]{4,3,2,1,0:T(8,128)(2,1)} %shard_map.37) | data formatting | bytes 8388608
Async XLA Ops:
  0.8 1.6 %copy-start = (bf16[1,128,32,2,128]{4,3,2,1,0:T(2,128)(2,1)S(1)}, bf16[1,128,32,2,128]{4,3,2,1,0:T(2,128)(2,1)}, u32[]{:S(2)}) copy-start(bf16[1,128,32,2,128]{4,3,2,1,0:T(2,128)(2,1)} %param.3) | copy-start | bytes 6291460
  2.4 0.7 copy-start.1

commit v2 on v1

--- a/solution.py
+++ b/solution.py
@@ -10,6 +10,7 @@
 NSAMP = 256
 EPS = 1e-06
 LANES = 128
+AHEAD = 2
 MESH = pl.DeviceIdType.MESH
 
 
@@ -24,9 +25,9 @@
 
 def kernel(cfg, x_ref, counts_ref, partner_ref, out_ref, *scratch):
     nchan, groups, nsub, per_sub, chosen, rounds, windows, width = cfg
-    (send, tall, raw, wgt, inv, stage, sem_as, sem_ar, sem_ys, sem_yr, sem_bs, sem_br,
-     sem_cs, sem_cr, sem_ts, sem_tr, sem_out) = scratch[:17]
-    held = scratch[17:]
+    (send, tall, raw, cts, wgt, inv, sem_as, sem_ar, sem_ys, sem_yr, sem_bs, sem_br,
+     sem_cs, sem_cr, sem_ts, sem_tr) = scratch[:16]
+    held = scratch[16:]
     bins = nsub * per_sub
     total_bins = nchan * bins
     me = lax.axis_index("chan")
@@ -69,10 +70,6 @@
             src_ref=tall.at[mine], dst_ref=tall.at[mine],
             send_sem=sem_ts.at[d], recv_sem=sem_tr.at[d],
             device_id={"win": flip(mine, d)}, device_id_type=MESH)
-
-    def store_out(s):
-        return pltpu.make_async_copy(
-            stage.at[s], out_ref.at[:, :, pl.ds(s * per_sub, per_sub)], sem_out.at[s])
 
     def add_power(f, acc):
         v = x_ref[f].astype(jnp.float32)
@@ -96,38 +93,37 @@
         lax.fori_loop(0, nchan, one, 0)
         held[s][me, mine] = send[s, me]
 
-    tall[mine] = jnp.zeros((windows, LANES), jnp.float32)
-    tall[mine, :, pl.ds(0, counts_ref.shape[1])] = counts_ref[...].astype(jnp.float32)
+    tall[mine] = jnp.zeros(tall.shape[1:], jnp.float32)
+    tall[mine, :, pl.ds(0, windows)] = counts_ref[...].astype(jnp.float32)
 
     whiten(0)
     pl.semaphore_wait(barrier, nchan - 1 + groups - 1)
+    to_across(0, 0).start()
+    to_beside(0, 0).start()
     for d in range(nchan - 1, 0, -1):
         to_bins(0, d).start()
     for d in range(1, groups):
         tallies(d).start()
-    for s in range(1, nsub):
+    for s in range(1, AHEAD):
         whiten(s)
-        if s < AHEAD:
-            for d in range(nchan - 1, 0, -1):
-                to_bins(s, d).start()
+        for d in range(nchan - 1, 0, -1):
+            to_bins(s, d).start()
 
     def weights():
         for d in range(1, groups):
             tallies(d).wait_recv()
-        c = tall[...].reshape(groups * windows, LANES)
-        lane = lax.broadcasted_iota(jnp.int32, c.shape, 1)
+        whole = tall[0]
+        for g in range(1, groups):
+            whole = whole + pltpu.roll(tall[g], g * windows, 1)
+        cts[...] = whole
         first = mine * chosen
 
-        def column(a):
-            return jnp.sum(jnp.where(lane == a, c, 0.0), axis=1, keepdims=True)
-
         def one(n, carry):
-            own = column(first + n)
+            own = cts[pl.ds(first + n, 1), :]
             for r in range(rounds):
-                w = jnp.minimum(own, column(partner_ref[r, first + n])) * (1.0 / NSAMP)
-                w = jnp.broadcast_to(w, (groups * windows, width))
-                wgt[n, r] = w.astype(jnp.bfloat16)
-                norm = lax.rsqrt(jnp.sum(w * w, axis=0, keepdims=True))
+                row = jnp.minimum(own, cts[pl.ds(partner_ref[r, first + n], 1), :]) * (1.0 / NSAMP)
+                wgt[n, r] = jnp.broadcast_to(row, (LANES, LANES)).T.astype(jnp.bfloat16)
+                norm = lax.rsqrt(jnp.sum(row * row, axis=1, keepdims=True))
                 inv[n, r] = jnp.broadcast_to(norm, (8, width))
             return carry
 
@@ -158,46 +154,50 @@
             norm = inv[n, r, pl.ds(0, 1), :]
             for k in range(2):
                 tile = res[k * width:(k + 1) * width, r * width:(r + 1) * width] * norm
-                stage[s, n, r, q, :, pl.ds(k * width, width)] = tile.astype(jnp.bfloat16)
+                out_ref[n, r, s * per_sub + q, :, pl.ds(k * width, width)] = tile.astype(jnp.bfloat16)
 
     units = chosen * per_sub
 
     def compute(s, low, high):
-        lax.fori_loop(low, high, lambda u, carry: (unit(s, u), carry)[1], 0)
+        lax.fori_loop(low, high, lambda u, carry: (unit(s, u), carry)[1], 0, unroll=2 if (high - low) % 2 == 0 else 1)
 
     def settle(s):
         for d in range(nchan):
             to_beside(s, d).wait_recv()
             relay(s, d).wait_recv()
 
-    late = nchan // 2
-    previous = None
+    def pass_on(step):
+        s, d = step // nchan, step % nchan
+        to_across(s, d).wait_recv()
+        relay(s, d).start()
+
+    lag = nchan // 2
+    late = 5 * nchan // 8
     for s in range(nsub):
         for d in range(nchan):
+            step = s * nchan + d
             if d:
                 to_bins(s, d).wait_recv()
-            to_across(s, d).start()
-            to_beside(s, d).start()
+            if step:
+                to_across(s, d).start()
+                to_beside(s, d).start()
+            if d == 0 and s + AHEAD < nsub:
+                whiten(s + AHEAD)
             if d and s + AHEAD < nsub:
                 to_bins(s + AHEAD, nchan - d).start()
-            if previous is not None:
-                to_across(*previous).wait_recv()
-                relay(*previous).start()
-            previous = (s, d)
-            if s == 0 and d == nchan - 1:
+            if step >= lag:
+                pass_on(step - lag)
+            if step == nchan - 1:
                 weights()
             if s and d >= late:
                 if d == late:
                     settle(s - 1)
-                step = d - late
-                compute(s - 1, step * units // (nchan - late), (step + 1) * units // (nchan - late))
-        if s:
-            store_out(s - 1).start()
-    to_across(*previous).wait_recv()
-    relay(*previous).start()
+                i = d - late
+                compute(s - 1, i * units // (nchan - late), (i + 1) * units // (nchan - late))
+    for step in range(nsub * nchan - lag, nsub * nchan):
+        pass_on(step)
     settle(nsub - 1)
     compute(nsub - 1, 0, units)
-    store_out(nsub - 1).start()
 
     for d in range(1, groups):
         tallies(d).wait_send()
@@ -208,11 +208,6 @@
             to_across(s, d).wait_send()
             to_beside(s, d).wait_send()
             relay(s, d).wait_send()
-    for s in range(nsub):
-        store_out(s).wait()
-
-
-AHEAD = 2
 
 
 def per_device(nchan, groups, spectra, counts, partner):
@@ -234,23 +229,22 @@
             pl.BlockSpec(memory_space=pltpu.VMEM),
             pl.BlockSpec(memory_space=pltpu.SMEM),
         ],
-        out_specs=pl.BlockSpec(memory_space=pl.ANY),
+        out_specs=pl.BlockSpec(memory_space=pltpu.VMEM),
         scratch_shapes=[
             pltpu.VMEM((nsub, nchan, per_sub, 2 * windows, width), jnp.bfloat16),
-            pltpu.VMEM((groups, windows, LANES), jnp.float32),
+            pltpu.VMEM((groups, nblocks, LANES), jnp.float32),
             pltpu.VMEM((per_sub, 2 * windows, width), jnp.float32),
+            pltpu.VMEM((nblocks, LANES), jnp.float32),
             pltpu.VMEM((chosen, rounds, groups * windows, width), jnp.bfloat16),
             pltpu.VMEM((chosen, rounds, 8, width), jnp.float32),
-            pltpu.VMEM((nsub, chosen, rounds, per_sub, width, 2 * width), jnp.bfloat16),
         ]
         + [dma((nsub, nchan))] * 8
         + [dma((groups,))] * 2
-        + [dma((nsub,))]
         + [pltpu.VMEM((nblocks, groups, per_sub, 2 * windows, width), jnp.bfloat16)] * nsub,
         compiler_params=pltpu.CompilerParams(
-            collective_id=0, has_side_effects=True, vmem_limit_bytes=48 * 1024 * 1024),
+            collective_id=0, has_side_effects=True, vmem_limit_bytes=40 * 1024 * 1024),
         cost_estimate=pl.CostEstimate(flops=flops, bytes_accessed=8 << 20, transcendentals=0),
-    )(x, counts, partner)
+    )(x, counts.T, partner)
 
 
 def solution(mesh):

time: 96.6 us -> 79.9 us (0.83)
  Pallas kernels: 88.7 us -> 74.8 us
  local copies, waits for them, and re-layouts: 7.73 us -> 4.97 us
    pallas_call x1, Pallas kernels: 88.7 us -> 74.8 us  [per_device(): pl.pallas_call(functools.partial(kernel, cfg), out_shape=jax.ShapeDtypeSt...]
    unnamed x6 -> x7, local copies, waits for them, and re-layouts: 7.73 us -> 4.97 us
where the time goes in v2:
time: 79.9 us; the launch traced here: 79.8 us
  Pallas kernels  74.8 us (94%)
  local copies, waits for them, and re-layouts  4.97 us (6%)
    pallas_call x1, Pallas kernels, per_device(): pl.pallas_call(functools.partial(kernel, cfg), out_shape=jax.ShapeDtypeSt...  74.8 us
    unnamed x7, local copies, waits for them, and re-layouts  4.97 us

profile of v2, /device:TPU:1, one launch (start us, length us, event | category | flops | bytes accessed | tf_op | source)
XLA Modules:
  0.0 79.8 jit_solution(6607260626453588917)
XLA Ops:
  0.0 0.0 copy-start
  0.0 1.6 %copy-done = bf16[1,128,32,2,128]{4,3,2,1,0:T(2,128)(2,1)S(1)} copy-done((bf16[1,128,32,2,128]{4,3,2,1,0:T(2,128)(2,1)S(1)}, bf16[1,128,32,2,128]{4,3,2,1,0:T(2,128)(2,1)}, u32[]{:S(2)}) %copy-start) | copy-done | bytes 2097176
  1.6 0.0 copy-start.1
  1.6 0.7 copy-done.1
  2.3 0.0 copy-start.2
  2.3 0.7 copy-done.2
  3.0 74.8 %shard_map.37 = bf16[2,2,16,128,256]{4,3,2,1,0:T(8,128)(2,1)S(1)} custom-call(bf16[128,64,128]{2,1,0:T(8,128)(2,1)S(1)} %bitcast.2, s32[8,32]{1,0:T(8,128)S(1)} %bitcast.3, s32[2,8]{1,0:T(2,128)S(1)} %copy-done.2), custom_call_target="tpu_custom_call" | custom-call | flops 1073741824 | bytes 8388608 | tf_op jit(solution)/shard_map/pallas_call | solution.py:224
  77.7 2.0 %copy.5 = bf16[2,2,16,128,256]{4,3,2,1,0:T(8,128)(2,1)} copy(bf16[2,2,16,128,256]{4,3,2,1,0:T(8,128)(2,1)S(1)} %shard_map.37) | data formatting | bytes 8388608
Async XLA Ops:
  0.0 1.6 %copy-start = (bf16[1,128,32,2,128]{4,3,2,1,0:T(2,128)(2,1)S(1)}, bf16[1,128,32,2,128]{4,3,2,1,0:T(2,128)(2,1)}, u32[]{:S(2)}) copy-start(bf16[1,128,32,2,128]{4,3,2,1,0:T(2,128)(2,1)} %param.3) | copy-start | bytes 6291460
  1.6 0.7 copy-start.1
  2.3 0.7 copy-start.2
